TPU v7x, 256 devices: a whole 4x4x8 slice. The times are simulated.
256 devices in a mesh: region: 128 (over x, z, y), batch: 2 (over core).
Axes of the slice: x: 4, y: 4, z: 8, core: 2. Of those that a mesh axis runs over, the one named last changes fastest.
Arguments:
- child_pixels: int32 [256, 1024], P('region', 'batch'), may hold values from 0 to 255
- parent_pixels: int32 [128, 1024], P('region', 'batch'), may hold values from 0 to 255
- child_leaf: bfloat16 [256, 1024, 256], P('region'), may hold values from -9 to 310
- parent_leaf: bfloat16 [128, 1024, 256], P('region'), may hold values from -9 to 9
- edge_weights: bfloat16 [256, 1024, 1024], P('region'), may hold values from 1.3671875e-08 to 0.12890625
- parent_of: int32 [256], replicated, may hold values from 0 to 127, as said below
- parent_flows: bfloat16 [128, 1024, 1024], P('region', 'batch'), may hold values from 0.049804688 to 1
Outputs:
- parent_ll: float32 [128, 1024, 1024], P('region', 'batch')
- child_flows: bfloat16 [256, 1024, 1024], P('region', 'batch')
- new_weights: bfloat16 [256, 1024, 1024], P('region', 'batch')
Inputs may be any that keep to these rules, and one draw needn't show every extreme that they name: `parent_of`: child c's parent is c // 2 - 1, c // 2 or c // 2 + 1.
All inputs are finite; a program needn't handle non-finite values.
Results may differ from a plain program's by a relative error of at most 0.012.
Values may be sent and summed in bfloat16 or wider, within the bound.
No kernel may reach another device: no remote copies, remote signals or barrier semaphores. Data moves between devices by JAX's collectives and lax.ppermute only.
A program may use at most 128 MiB of HBM per device.

v0:
```python
import jax
import jax.numpy as jnp
from jax import lax
from jax.sharding import PartitionSpec as P

PRIOR = 0.05


def with_halo(array, sides, width):
    for axis, dim in sides:
        peers, length = (lax.axis_size(axis), array.shape[dim])
        up = [(i, (i + 1) % peers) for i in range(peers - 1)]
        down = [(j, i) for i, j in up]
        last = lax.slice_in_dim(array, length - width, length, axis=dim)
        first = lax.slice_in_dim(array, 0, width, axis=dim)
        before = lax.ppermute(last, axis, up)
        after = lax.ppermute(first, axis, down)
        array = jnp.concatenate([before, array, after], axis=dim)
    return array


def lookup_rows(leaf, pixels):
    table = jnp.transpose(jax.nn.log_softmax(leaf.astype(jnp.float32), axis=-1), (0, 2, 1))

    def one_region(region_table, region_pixels):
        return region_table[region_pixels]

    return jax.vmap(one_region)(table, pixels)


def on_device(
    child_pixels, parent_pixels, child_leaf, parent_leaf, edge_weights, parent_of, parent_flows
):
    position = lax.axis_index("region")
    child_count = edge_weights.shape[0]
    states = edge_weights.shape[1]
    own_parents = lax.dynamic_slice_in_dim(parent_of, position * child_count, child_count)
    offset = own_parents - position
    loglik = lookup_rows(child_leaf, child_pixels)
    row_peak = jnp.max(loglik, axis=-1, keepdims=True)
    shifted = jnp.exp(loglik - row_peak).astype(jnp.bfloat16)
    totals = jnp.einsum("cbj,ckj->cbk", shifted, edge_weights, preferred_element_type=jnp.float32)
    message = row_peak + jnp.log(totals)
    nearby = with_halo(message.astype(jnp.bfloat16), (("region", 0),), child_count).astype(
        message.dtype
    )
    filler = jnp.full((child_count,), -1, jnp.int32)
    padded_ids = jnp.concatenate([filler, parent_of, filler])
    near_ids = lax.dynamic_slice_in_dim(padded_ids, position * child_count, 3 * child_count)
    received = jnp.sum(
        jnp.where((near_ids == position)[:, None, None], nearby, 0.0), axis=0, keepdims=True
    )
    parent_ll = lookup_rows(parent_leaf, parent_pixels) + received
    flow_rim = with_halo(parent_flows, (("region", 0),), 1)
    upstream = jnp.take(flow_rim, offset + 1, axis=0).astype(jnp.float32)
    scaled = (upstream / totals).astype(jnp.bfloat16)
    pulled_back = jnp.einsum(
        "cbk,ckj->cbj", scaled, edge_weights, preferred_element_type=jnp.float32
    )
    child_flows = (shifted.astype(jnp.float32) * pulled_back).astype(jnp.bfloat16)
    pair_counts = jnp.einsum("cbk,cbj->ckj", scaled, shifted, preferred_element_type=jnp.float32)
    row_count = states // lax.axis_size("batch")
    row_start = lax.axis_index("batch") * row_count
    summed_all = lax.psum(pair_counts.astype(jnp.bfloat16), "batch").astype(jnp.float32)
    summed = lax.dynamic_slice_in_dim(summed_all, row_start, row_count, 1)
    weight_rows = lax.dynamic_slice_in_dim(edge_weights, row_start, row_count, 1).astype(
        jnp.float32
    )
    counts = weight_rows * summed + PRIOR
    new_weights = (states * counts / jnp.sum(counts, axis=-1, keepdims=True)).astype(jnp.bfloat16)
    return (parent_ll, child_flows, new_weights)


def solution(mesh):
    return jax.shard_map(
        on_device,
        mesh=mesh,
        in_specs=(
            P("region", "batch"),
            P("region", "batch"),
            P("region", None, None),
            P("region", None, None),
            P("region", None, None),
            P(),
            P("region", "batch", None),
        ),
        out_specs=(
            P("region", "batch", None),
            P("region", "batch", None),
            P("region", "batch", None),
        ),
        check_vma=False,
    )
```

profile of v0, /device:TPU:5, one launch (start us, length us, event | category | flops | bytes accessed | tf_op | source)
XLA Modules:
  0.0 136.6 jit_solution(487876165896487514)
XLA Ops:
  7.2 0.0 all-reduce.2.cloned.1.call-start
  7.2 3.2 %collective-permute-start.2 = (bf16[1,512,1024]{2,1,0:T(8,128)(2,1)}, bf16[1,512,1024]{2,1,0:T(8,128)(2,1)}, u32[]{:S(2)}, u32[]{:S(2)}) collective-permute-start(bf16[1,512,1024]{2,1,0:T(8,128)(2,1)} %param.13), channel_id=1, source_target_pairs={{0,2},{2,4},{4,6},{6,8},{8,10},{10,12},{12,14},{14,16},{16,18},{18... | collective-permute-start | bytes 3145736 | tf_op jit(solution)/shard_map/ppermute | solution.py:16
  10.4 8.6 %collective-permute-start.3 = (bf16[1,512,1024]{2,1,0:T(8,128)(2,1)}, bf16[1,512,1024]{2,1,0:T(8,128)(2,1)}, u32[]{:S(2)}, u32[]{:S(2)}) collective-permute-start(bf16[1,512,1024]{2,1,0:T(8,128)(2,1)} %param.13), channel_id=1, source_target_pairs={{2,0},{4,2},{6,4},{8,6},{10,8},{12,10},{14,12},{16,14},{18,16},{20... | collective-permute-start | bytes 3145736 | tf_op jit(solution)/shard_map/ppermute | solution.py:17
  19.1 1.5 %copy.14 = bf16[2,1024,256]{1,2,0:T(8,128)(2,1)S(1)} copy(bf16[2,1024,256]{2,1,0:T(8,128)(2,1)} %param.9) | data formatting | bytes 2097152 | tf_op args[2]
  20.6 1.5 %reduce_max.41 = bf16[2,1024]{1,0:T(2,128)(2,1)S(1)} reduce(bf16[2,1024,256]{2,1,0:T(8,128)(2,1)} %param.9, bf16[]{:T(256)} %constant.18.clone.1), dimensions={2}, to_apply=%region_2.3 | reduce | flops 522240 | bytes 1052674 | tf_op jit(solution)/shard_map/jit(log_softmax)/reduce_max | solution.py:23
  22.1 0.1 compare_and_fusion
  22.2 1.4 %fusion.3 = f32[2,256,1024]{2,1,0:T(8,128)S(1)} fusion(bf16[2,1024,256]{1,2,0:T(8,128)(2,1)S(1)} %copy.14, f32[2,1024]{1,0:T(2,128)S(1)} %reduce_max.42), kind=kOutput, calls=%fused_computation.16 | output fusion | flops 2623743 | bytes 3153920 | tf_op jit(solution)/shard_map/jit(log_softmax)/reduce_sum | solution.py:23
  23.6 14.9 %gather_fusion.2 = f32[1024,1024]{1,0:T(8,128)} fusion(f32[2,256,1024]{2,1,0:T(8,128)S(1)} %fusion.3, s32[1024]{0:T(1024)S(1)} %bitcast.28), kind=kCustom, calls=%fused_computation.2 | custom fusion | bytes 8396800 | tf_op jit(solution)/shard_map/vmap()/gather | solution.py:26
  38.5 2.4 %reduce.4 = f32[1024]{0:T(1024)S(1)} reduce(f32[1024,1024]{1,0:T(8,128)} %gather_fusion.2, f32[]{:T(128)} %constant.33.clone.1), dimensions={1}, to_apply=%region_4.5 | reduce | flops 1047552 | bytes 4198404 | tf_op jit(solution)/shard_map/reduce_max | solution.py:40
  41.0 3.0 %exponential_convert_fusion = bf16[2,512,1024]{2,1,0:T(8,128)(2,1)S(1)} fusion(f32[2,512,1024]{2,1,0:T(8,128)} %bitcast.29, f32[2,512]{1,0:T(2,128)S(1)} %reshape.75), kind=kLoop, calls=%fused_computation.11 | loop fusion | flops 2097152 | bytes 6295552 | tf_op jit(solution)/shard_map/convert_element_type | solution.py:41
  43.9 0.5 copy-done.8
  44.4 4.3 %fusion.22 = f32[2,512,1024]{2,1,0:T(8,128)} fusion(bf16[2,512,1024]{2,1,0:T(8,128)(2,1)S(1)} %exponential_convert_fusion, bf16[2,1024,1024]{2,1,0:T(8,128)(2,1)S(1)} %copy-done.8), kind=kOutput, calls=%fused_computation.49 | convolution fusion | flops 2147483648 | bytes 10485760 | tf_op jit(solution)/shard_map/cbj,ckj->cbk/dot_general | solution.py:42
  48.8 1.9 %pad_maximum_fusion = bf16[3,512,1024]{2,1,0:T(8,128)(2,1)S(1)} fusion(bf16[1,512,1024]{2,1,0:T(8,128)(2,1)} %collective-permute-done.3, bf16[1,512,1024]{2,1,0:T(8,128)(2,1)S(1)} %copy-done.4, bf16[1,512,1024]{2,1,0:T(8,128)(2,1)} %collective-permute-done.2), kind=kLoop, calls=%fused_computation.13 | loop fusion | flops 3145728 | bytes 6291456 | tf_op jit(solution)/shard_map/concatenate | solution.py:18
  50.6 2.0 %gather_fusion = bf16[2,512,1024]{2,1,0:T(8,128)(2,1)} fusion(bf16[3,512,1024]{2,1,0:T(8,128)(2,1)S(1)} %pad_maximum_fusion, s32[1024]{0:T(1024)S(1)} %pad_clamp_fusion), kind=kCustom, calls=%fused_computation | custom fusion | bytes 4194312 | tf_op jit(solution)/shard_map/jit(_take)/gather | solution.py:55
  52.6 4.5 %divide_convert_fusion.1 = (bf16[2,512,1024]{2,1,0:T(8,128)(2,1)S(1)}, bf16[2,512,1024]{2,1,0:T(8,128)(2,1)}) fusion(f32[2,512,1024]{2,1,0:T(8,128)} %fusion.22, bf16[2,512,1024]{2,1,0:T(8,128)(2,1)} %gather_fusion, pred[2]{0:T(512)(128)(4,1)S(1)} %get-tuple-element.3, f32[2,512]{1,0:T(2,128)S(1)} %reshape.75), kind=kLoop, calls=%fused_computation.9 | loop fusion | flops 6291456 | bytes 10489858 | tf_op jit(solution)/shard_map/convert_element_type | solution.py:56
  57.2 1.3 copy-done
  58.5 4.4 %convolution_convert_fusion = bf16[2,1024,1024]{2,1,0:T(8,128)(2,1)} fusion(bf16[2,512,1024]{2,1,0:T(8,128)(2,1)S(1)} %get-tuple-element.5, bf16[2,512,1024]{2,1,0:T(8,128)(2,1)S(1)} %copy-done.3), kind=kOutput, calls=%fused_computation.14 | convolution fusion | flops 2149580800 | bytes 8388608 | tf_op jit(solution)/shard_map/cbk,cbj->ckj/dot_general | solution.py:61
  62.9 2.1 %collective-permute-start = (bf16[2,512,1024]{2,1,0:T(8,128)(2,1)}, bf16[2,512,1024]{2,1,0:T(8,128)(2,1)}, u32[]{:S(2)}, u32[]{:S(2)}) collective-permute-start(bf16[2,512,1024]{2,1,0:T(8,128)(2,1)} %get-tuple-element.6), channel_id=1, source_target_pairs={{0,2},{2,4},{4,6},{6,8},{8,10},{10,12},{12,14},{14,16},{16,18},{18... | collective-permute-start | bytes 6291464 | tf_op jit(solution)/shard_map/ppermute | solution.py:16
  65.0 7.8 %collective-permute-start.1 = (bf16[2,512,1024]{2,1,0:T(8,128)(2,1)}, bf16[2,512,1024]{2,1,0:T(8,128)(2,1)}, u32[]{:S(2)}, u32[]{:S(2)}) collective-permute-start(bf16[2,512,1024]{2,1,0:T(8,128)(2,1)} %get-tuple-element.6), channel_id=1, source_target_pairs={{2,0},{4,2},{6,4},{8,6},{10,8},{12,10},{14,12},{16,14},{18,16},{20... | collective-permute-start | bytes 6291464 | tf_op jit(solution)/shard_map/ppermute | solution.py:17
  72.7 0.2 copy.13
  73.0 0.2 reduce_max.39
  73.1 0.2 exponential_reduce_fusion.1
  73.4 0.1 subtract_bitcast_fusion
  73.5 3.7 %gather_fusion.1 = f32[512,1024]{1,0:T(8,128)S(1)} fusion(f32[1,256,1024]{2,1,0:T(8,128)S(1)} %subtract_bitcast_fusion, s32[512]{0:T(512)S(1)} %bitcast.30), kind=kCustom, calls=%fused_computation.1 | custom fusion | bytes 4198400 | tf_op jit(solution)/shard_map/vmap()/gather | solution.py:26
  77.2 0.1 pad_add_fusion
  77.3 0.1 dynamic-slice_compare_fusion
  77.4 7.3 %multiply_convert_fusion = bf16[2,512,1024]{2,1,0:T(8,128)(2,1)} fusion(bf16[2,512,1024]{2,1,0:T(8,128)(2,1)} %copy-done.2, bf16[2,512,1024]{2,1,0:T(8,128)(2,1)} %copy-done, bf16[2,1024,1024]{2,1,0:T(8,128)(2,1)} %param.11), kind=kOutput, calls=%fused_computation.8 | convolution fusion | flops 2150629376 | bytes 10485760 | tf_op jit(solution)/shard_map/cbk,ckj->cbj/dot_general | solution.py:57
  84.6 31.0 %collective-permute-done = bf16[2,512,1024]{2,1,0:T(8,128)(2,1)} collective-permute-done((bf16[2,512,1024]{2,1,0:T(8,128)(2,1)}, bf16[2,512,1024]{2,1,0:T(8,128)(2,1)}, u32[]{:S(2)}, u32[]{:S(2)}) %collective-permute-start) | collective-permute-done | bytes 2097184 | tf_op jit(solution)/shard_map/ppermute | solution.py:16
  115.6 0.9 collective-permute-done.1
  116.5 5.2 %select_reduce_fusion = f32[512,1024]{1,0:T(8,128)S(1)} fusion(bf16[2,512,1024]{2,1,0:T(8,128)(2,1)} %collective-permute-done.1, bf16[2,512,1024]{2,1,0:T(8,128)(2,1)} %get-tuple-element.6, bf16[2,512,1024]{2,1,0:T(8,128)(2,1)} %collective-permute-done, pred[6]{0:T(512)(128)(4,1)S(1)} %dynamic-slice_compare_fusion), kind=kLoop, calls=%fused_computation.5 | loop fusion | flops 15204352 | bytes 8388614 | tf_op jit(solution)/shard_map/reduce_sum | solution.py:50
  121.7 1.7 %add_bitcast_fusion = f32[1,512,1024]{2,1,0:T(8,128)} fusion(f32[512,1024]{1,0:T(8,128)S(1)} %gather_fusion.1, f32[512,1024]{1,0:T(8,128)S(1)} %select_reduce_fusion), kind=kLoop, calls=%fused_computation.17 | loop fusion | flops 524288 | bytes 6291456 | tf_op jit(solution)/shard_map/add | solution.py:53
  123.4 6.3 %divide_convert_fusion = bf16[2,512,1024]{2,1,0:T(8,128)(2,1)} fusion(bf16[2,1024,1024]{2,1,0:T(8,128)(2,1)} %all-reduce.2.cloned.1.call-done, s32[]{:T(128)S(6)} %select_n.36, bf16[2,1024,1024]{2,1,0:T(8,128)(2,1)} %param.11), kind=kOutput, calls=%fused_computation.6 | output fusion | flops 11536383 | bytes 10486784 | tf_op jit(solution)/shard_map/div | solution.py:70
  (31 shorter events, 0.1 us)
Async XLA Ops:
  7.2 14.9 %copy-start.5 = (s32[2,512]{1,0:T(2,128)S(1)}, s32[2,512]{1,0:T(2,128)}, u32[]{:S(2)}) copy-start(s32[2,512]{1,0:T(2,128)} %param.7) | copy-start | bytes 12292
  7.2 14.9 %copy-start.6 = (s32[256]{0:T(256)S(1)}, s32[256]{0:T(256)}, u32[]{:S(2)}) copy-start(s32[256]{0:T(256)} %param.12) | copy-start | bytes 3076
  7.2 116.3 %all-reduce.2.cloned.1.call-start = ((), (), s32[]{:S(2)}) async-start(), calls=%async_computation | async-start | bytes 8388608 | tf_op jit(solution)/shard_map/psum | solution.py:64
  7.2 41.5 %collective-permute-start.2 = (bf16[1,512,1024]{2,1,0:T(8,128)(2,1)}, bf16[1,512,1024]{2,1,0:T(8,128)(2,1)}, u32[]{:S(2)}, u32[]{:S(2)}) collective-permute-start(bf16[1,512,1024]{2,1,0:T(8,128)(2,1)} %param.13), channel_id=1, source_target_pairs={{0,2},{2,4},{4,6},{6,8},{8,10},{10,12},{12,14},{14,16},{16,18},{18... | collective-permute-start | bytes 3145736 | tf_op jit(solution)/shard_map/ppermute | solution.py:16
  10.4 38.3 %collective-permute-start.3 = (bf16[1,512,1024]{2,1,0:T(8,128)(2,1)}, bf16[1,512,1024]{2,1,0:T(8,128)(2,1)}, u32[]{:S(2)}, u32[]{:S(2)}) collective-permute-start(bf16[1,512,1024]{2,1,0:T(8,128)(2,1)} %param.13), channel_id=1, source_target_pairs={{2,0},{4,2},{6,4},{8,6},{10,8},{12,10},{14,12},{16,14},{18,16},{20... | collective-permute-start | bytes 3145736 | tf_op jit(solution)/shard_map/ppermute | solution.py:17
  41.0 3.5 %copy-start.8 = (bf16[2,1024,1024]{2,1,0:T(8,128)(2,1)S(1)}, bf16[2,1024,1024]{2,1,0:T(8,128)(2,1)}, u32[]{:S(2)}) copy-start(bf16[2,1024,1024]{2,1,0:T(8,128)(2,1)} %param.11) | copy-start | bytes 12582916
  44.4 4.3 %copy-start.2 = (bf16[2,512,1024]{2,1,0:T(8,128)(2,1)}, bf16[2,512,1024]{2,1,0:T(8,128)(2,1)S(1)}, u32[]{:S(2)}) copy-start(bf16[2,512,1024]{2,1,0:T(8,128)(2,1)S(1)} %exponential_convert_fusion) | copy-start | bytes 6291460
  44.4 4.3 %copy-start.4 = (bf16[1,512,1024]{2,1,0:T(8,128)(2,1)S(1)}, bf16[1,512,1024]{2,1,0:T(8,128)(2,1)}, u32[]{:S(2)}) copy-start(bf16[1,512,1024]{2,1,0:T(8,128)(2,1)} %param.13) | copy-start | bytes 3145732
  52.6 5.8 %copy-start.3 = (bf16[2,512,1024]{2,1,0:T(8,128)(2,1)S(1)}, bf16[2,512,1024]{2,1,0:T(8,128)(2,1)}, u32[]{:S(2)}) copy-start(bf16[2,512,1024]{2,1,0:T(8,128)(2,1)} %copy-done.2) | copy-start | bytes 6291460
  57.2 1.3 copy-start
  62.9 9.9 %copy-start.1 = (bf16[1,1024,256]{2,1,0:T(8,128)(2,1)S(1)}, bf16[1,1024,256]{2,1,0:T(8,128)(2,1)}, u32[]{:S(2)}) copy-start(bf16[1,1024,256]{2,1,0:T(8,128)(2,1)} %param.10) | copy-start | bytes 1572868
  62.9 10.5 %copy-start.7 = (s32[1,512]{1,0:T(1,128)S(1)}, s32[1,512]{1,0:T(1,128)}, u32[]{:S(2)}) copy-start(s32[1,512]{1,0:T(1,128)} %param.8) | copy-start | bytes 6148
  62.9 52.7 %collective-permute-start = (bf16[2,512,1024]{2,1,0:T(8,128)(2,1)}, bf16[2,512,1024]{2,1,0:T(8,128)(2,1)}, u32[]{:S(2)}, u32[]{:S(2)}) collective-permute-start(bf16[2,512,1024]{2,1,0:T(8,128)(2,1)} %get-tuple-element.6), channel_id=1, source_target_pairs={{0,2},{2,4},{4,6},{6,8},{8,10},{10,12},{12,14},{14,16},{16,18},{18... | collective-permute-start | bytes 6291464 | tf_op jit(solution)/shard_map/ppermute | solution.py:16
  65.0 51.6 %collective-permute-start.1 = (bf16[2,512,1024]{2,1,0:T(8,128)(2,1)}, bf16[2,512,1024]{2,1,0:T(8,128)(2,1)}, u32[]{:S(2)}, u32[]{:S(2)}) collective-permute-start(bf16[2,512,1024]{2,1,0:T(8,128)(2,1)} %get-tuple-element.6), channel_id=1, source_target_pairs={{2,0},{4,2},{6,4},{8,6},{10,8},{12,10},{14,12},{16,14},{18,16},{20... | collective-permute-start | bytes 6291464 | tf_op jit(solution)/shard_map/ppermute | solution.py:17
Sparse Core Ops, SparseCore 0:
  63.0 37.3 all-reduce.1
where the time goes:
time: 139 us; the launch traced here: 137 us
  waiting for transfers between devices  31.9 us (23%)
  other arithmetic  28.7 us (21%)
  local copies, waits for them, and re-layouts  24.1 us (17%)
  starting transfers between devices  21.7 us (16%)
  matrix products  16 us (12%)
  between operations  14.3 us (10%)
    ppermute x2, waiting for transfers between devices, with_halo(): before = lax.ppermute(last, axis, up)  31 us
    gather x3, local copies, waits for them, and re-layouts, one_region(): return region_table[region_pixels]  18.6 us
    ppermute x2, starting transfers between devices, with_halo(): after = lax.ppermute(first, axis, down)  16.4 us
    dot_general x1, matrix products, on_device(): jnp.einsum('cbk,ckj->cbj', scaled, edge_weights, preferred_element_type=j...  7.26 us
    div x1, other arithmetic, on_device(): states * counts / jnp.sum(counts, axis=-1, keepdims=True)  6.34 us
    ppermute x2, starting transfers between devices, with_halo(): before = lax.ppermute(last, axis, up)  5.26 us
    reduce_sum x1, other arithmetic, on_device(): jnp.sum(jnp.where((near_ids == position)[:, None, None], nearby, 0.0), ax...  5.18 us
    convert_element_type x1, other arithmetic, on_device(): scaled = (upstream / totals).astype(jnp.bfloat16)  4.51 us
  transfers between devices with their start and end apart: 5, of which 2 were waited for; matrix products, arithmetic and copies ran while one was open for 35% of the time, Pallas kernels for 0%

commit v1 on v0

v1 whole, which is shorter than its diff:
```python
import functools

import jax
import jax.numpy as jnp
from jax import lax
from jax.experimental import pallas as pl
from jax.experimental.pallas import tpu as pltpu
from jax.sharding import PartitionSpec as P

PRIOR = 0.05
F32, BF16 = jnp.float32, jnp.bfloat16
MIB = 2**20


def log_softmax_by_value(leaf):
    logits = jnp.transpose(leaf.astype(F32))
    top = jnp.max(logits, axis=0, keepdims=True)
    logits = logits - top
    return logits - jnp.log(jnp.sum(jnp.exp(logits), axis=0, keepdims=True))


def one_hot_rows(pixels, values):
    rows = lax.broadcasted_iota(jnp.int32, (values, pixels.shape[1]), 0)
    return jnp.where(rows == pixels, 1.0, 0.0).astype(F32)


def params(limit):
    return pltpu.CompilerParams(vmem_limit_bytes=limit * MIB)


def cost(flops, moved, exps=0):
    return pl.CostEstimate(flops=flops, bytes_accessed=moved, transcendentals=exps)


def tables_kernel(
    ids_ref, leaf_ref, weights_ref, mine_ref, theirs_ref, shifted_ref, inverse_ref, message_ref, sent_ref
):
    child = pl.program_id(0)
    table = log_softmax_by_value(leaf_ref[0])
    peak = jnp.max(table, axis=1, keepdims=True)
    shifted = jnp.exp(table - peak).astype(BF16)
    shifted_ref[0] = shifted
    totals = lax.dot_general(
        shifted, weights_ref[0], (((1,), (1,)), ((), ())), preferred_element_type=F32
    )
    inverse_ref[0] = (1.0 / totals).astype(BF16)
    message = (peak + jnp.log(totals)).astype(BF16)
    message_ref[0] = message
    values = message.shape[0]
    start = pl.multiple_of(child * values, values)
    sent_ref[pl.ds(start, values)] = message

    @pl.when(child == 0)
    def _():
        core = ids_ref[ids_ref.shape[0] - 1]
        own = jnp.concatenate([mine_ref[c] for c in range(mine_ref.shape[0])], axis=1)
        other = jnp.concatenate([theirs_ref[c] for c in range(mine_ref.shape[0])], axis=1)
        half = lax.broadcasted_iota(jnp.int32, (16, own.shape[1]), 0)
        rows = jnp.where(half == core, own, other).astype(F32).astype(BF16)
        sent_ref[sent_ref.shape[0] - 16 :] = rows


def tables(ids, leaf, weights, mine, theirs):
    children, states, values = leaf.shape
    one = lambda *block: pl.BlockSpec((1, *block), lambda c, ids: (c, 0, 0))
    pixels = pl.BlockSpec(mine.shape, lambda c, ids: (0, 0, 0))
    rows = children * values + 16
    return pl.pallas_call(
        tables_kernel,
        grid_spec=pltpu.PrefetchScalarGridSpec(
            num_scalar_prefetch=1,
            grid=(children,),
            in_specs=[one(states, values), one(states, states), pixels, pixels],
            out_specs=[one(values, states)] * 3
            + [pl.BlockSpec((rows, states), lambda c, ids: (0, 0))],
        ),
        out_shape=[jax.ShapeDtypeStruct((children, values, states), BF16)] * 3
        + [jax.ShapeDtypeStruct((rows, states), BF16)],
        compiler_params=params(60),
        cost_estimate=cost(2 * children * values * states**2, 12 * MIB),
        name="tables",
    )(ids, leaf, weights, mine, theirs)


def after(value, *others):
    anywhere = pl.BlockSpec(memory_space=pl.ANY)
    return pl.pallas_call(
        lambda *refs: None,
        in_specs=[anywhere] * (1 + len(others)),
        out_specs=anywhere,
        out_shape=jax.ShapeDtypeStruct(value.shape, value.dtype),
        input_output_aliases={0: 0},
        compiler_params=params(60),
        cost_estimate=cost(0, 0),
        name="after",
    )(value, *others)


def home_kernel(ids_ref, parent_pix_ref, child_pix_ref, leaf_ref, message_ref, out_ref):
    position = ids_ref[ids_ref.shape[0] - 2]
    children, values, _ = message_ref.shape
    logits = leaf_ref[0]
    wide = logits.astype(F32)
    top = jnp.max(wide, axis=1, keepdims=True)
    norm = top + jnp.log(jnp.sum(jnp.exp(wide - top), axis=1, keepdims=True))
    norm_row = jnp.transpose(jnp.broadcast_to(norm, (norm.shape[0], 128)))[:1]
    hot = jnp.transpose(one_hot_rows(parent_pix_ref[0], values)).astype(BF16)
    total = (
        lax.dot_general(hot, logits, (((1,), (1,)), ((), ())), preferred_element_type=F32)
        - norm_row
    )
    for c in range(children):
        mine = jnp.where(ids_ref[position * children + c] == position, 1.0, 0.0)
        hot = jnp.transpose(one_hot_rows(child_pix_ref[c], values) * mine).astype(BF16)
        total = total + jnp.dot(hot, message_ref[c], preferred_element_type=F32)
    out_ref[0] = total


def home(ids, parent_pix, child_pix, leaf, message):
    children, values, states = message.shape
    samples = parent_pix.shape[2]
    whole = lambda shape: pl.BlockSpec(shape, lambda i, ids: (0,) * len(shape))
    return pl.pallas_call(
        home_kernel,
        grid_spec=pltpu.PrefetchScalarGridSpec(
            num_scalar_prefetch=1,
            grid=(1,),
            in_specs=[whole(a.shape) for a in (parent_pix, child_pix, leaf, message)],
            out_specs=whole((1, samples, states)),
        ),
        out_shape=jax.ShapeDtypeStruct((1, samples, states), F32),
        compiler_params=params(60),
        cost_estimate=cost(6 * samples * states * values, 4 * MIB),
        name="home",
    )(ids, parent_pix, child_pix, leaf, message)


def flows_kernel(
    ids_ref, pix_ref, before_ref, here_ref, after_ref, shifted_ref, inverse_ref, weights_ref,
    flows_ref, sums_ref,
):
    child, part = pl.program_id(0), pl.program_id(1)
    position = ids_ref[ids_ref.shape[0] - 2]
    source = ids_ref[position * pl.num_programs(0) + child] - position
    above = jnp.where(
        source == 0, here_ref[0], jnp.where(source < 0, before_ref[0], after_ref[0])
    )
    values = shifted_ref.shape[1]
    hot_rows = one_hot_rows(pix_ref[0], values)
    hot = jnp.transpose(hot_rows).astype(BF16)
    inverse = jnp.dot(hot, inverse_ref[0], preferred_element_type=F32)
    scaled = (above.astype(F32) * inverse).astype(BF16)
    pulled = jnp.dot(scaled, weights_ref[0], preferred_element_type=F32)
    shifted = jnp.dot(hot, shifted_ref[0], preferred_element_type=F32)
    flows_ref[0] = (shifted * pulled).astype(BF16)
    sums = jnp.dot(hot_rows.astype(BF16), above, preferred_element_type=F32)

    @pl.when(part == 0)
    def _():
        sums_ref[0] = sums

    @pl.when(part > 0)
    def _():
        sums_ref[0] += sums


def flows(ids, pix, before, here, after, shifted, inverse, weights):
    children, values, states = shifted.shape
    samples = here.shape[1]
    rows = samples // 2
    near = pl.BlockSpec((1, rows, states), lambda c, i, ids: (0, i, 0))
    one = lambda *block: pl.BlockSpec((1, *block), lambda c, i, ids: (c, 0, 0))
    return pl.pallas_call(
        flows_kernel,
        grid_spec=pltpu.PrefetchScalarGridSpec(
            num_scalar_prefetch=1,
            grid=(children, samples // rows),
            in_specs=[
                pl.BlockSpec((1, 1, rows), lambda c, i, ids: (c, 0, i)),
                near,
                near,
                near,
                one(values, states),
                one(values, states),
                one(states, states),
            ],
            out_specs=[
                pl.BlockSpec((1, rows, states), lambda c, i, ids: (c, i, 0)),
                one(values, states),
            ],
        ),
        out_shape=[
            jax.ShapeDtypeStruct((children, samples, states), BF16),
            jax.ShapeDtypeStruct((children, values, states), F32),
        ],
        compiler_params=params(60),
        cost_estimate=cost(2 * children * samples * states * (states + 3 * values), 12 * MIB),
        name="flows",
    )(ids, pix, before, here, after, shifted, inverse, weights)


def update_kernel(ids_ref, mine_ref, theirs_ref, inverse_ref, shifted_ref, weights_ref, out_ref):
    sums = (mine_ref[0] + theirs_ref[0].astype(F32)) * inverse_ref[0].astype(F32)
    pairs = jnp.dot(
        jnp.transpose(sums).astype(BF16), shifted_ref[0], preferred_element_type=F32
    )
    counts = weights_ref[0].astype(F32) * pairs + PRIOR
    scale = counts.shape[1] / jnp.sum(counts, axis=1, keepdims=True)
    out_ref[0] = (counts * scale).astype(BF16)


def update(ids, sums, theirs, inverse, shifted, weights):
    children, values, states = shifted.shape
    rows = theirs.shape[2]
    core = ids.shape[0] - 1
    return pl.pallas_call(
        update_kernel,
        grid_spec=pltpu.PrefetchScalarGridSpec(
            num_scalar_prefetch=1,
            grid=(children,),
            in_specs=[
                pl.BlockSpec((1, values, rows), lambda c, ids: (c, 0, ids[core])),
                pl.BlockSpec((1, values, rows), lambda c, ids: (c, 0, 0)),
                pl.BlockSpec((1, values, rows), lambda c, ids: (c, 0, ids[core])),
                pl.BlockSpec((1, values, states), lambda c, ids: (c, 0, 0)),
                pl.BlockSpec((1, rows, states), lambda c, ids: (c, ids[core], 0)),
            ],
            out_specs=pl.BlockSpec((1, rows, states), lambda c, ids: (c, 0, 0)),
        ),
        out_shape=jax.ShapeDtypeStruct((children, rows, states), BF16),
        compiler_params=params(60),
        cost_estimate=cost(2 * children * rows * states * values, 8 * MIB),
        name="update",
    )(ids, sums, theirs, inverse, shifted, weights)


def gather_kernel(children, ids_ref, landed_ref, other_ref, sofar_ref, out_ref):
    count = ids_ref.shape[0] - 2
    position, core = ids_ref[count], ids_ref[count + 1]
    samples = out_ref.shape[1]
    values = (landed_ref.shape[0] - 16) // children
    total = sofar_ref[0]
    for table_ref, from_low in ((landed_ref, core == 0), (other_ref, core == 1)):
        halves = table_ref[children * values :].astype(F32)
        pixels = jnp.where(core == 0, halves[0:1], halves[1:2]).astype(jnp.int32)
        neighbour = jnp.where(from_low, position - 1, position + 1)
        for c in range(children):
            child = neighbour * children + c
            there = jnp.logical_and(child >= 0, child < count)
            parent = ids_ref[jnp.clip(child, 0, count - 1)]
            mine = jnp.where(jnp.logical_and(there, parent == position), 1.0, 0.0)
            hot = one_hot_rows(pixels[:, c * samples : (c + 1) * samples], values)
            hot = jnp.transpose(hot * mine).astype(BF16)
            table = table_ref[c * values : (c + 1) * values]
            total = total + jnp.dot(hot, table, preferred_element_type=F32)
    out_ref[0] = total


def gather(children, ids, landed, other, sofar):
    whole = lambda shape: pl.BlockSpec(shape, lambda i, ids: (0,) * len(shape))
    return pl.pallas_call(
        functools.partial(gather_kernel, children),
        grid_spec=pltpu.PrefetchScalarGridSpec(
            num_scalar_prefetch=1,
            grid=(1,),
            in_specs=[whole(a.shape) for a in (landed, other, sofar)],
            out_specs=whole(sofar.shape),
        ),
        out_shape=jax.ShapeDtypeStruct(sofar.shape, F32),
        input_output_aliases={3: 0},
        compiler_params=params(60),
        cost_estimate=cost(2 * sofar.shape[1] * landed.shape[0] * landed.shape[1], 6 * MIB),
        name="gather",
    )(ids, landed, other, sofar)


def on_device(
    child_pixels, parent_pixels, child_leaf, parent_leaf, edge_weights, parent_of, parent_flows
):
    regions, cores = lax.axis_size("region"), lax.axis_size("batch")
    position, core = lax.axis_index("region"), lax.axis_index("batch")
    up = [(i, i + 1) for i in range(regions - 1)]
    down = [(i + 1, i) for i in range(regions - 1)]
    swap = [(0, 1), (1, 0)]
    children, samples = child_pixels.shape
    states = edge_weights.shape[1]
    ids = jnp.concatenate([parent_of, jnp.stack([position, core]).astype(jnp.int32)])
    child_pix = child_pixels[:, None, :]
    low = lax.ppermute(parent_flows, "region", up)
    high = lax.ppermute(parent_flows, "region", down)
    other_pix = lax.ppermute(child_pixels, "batch", swap)[:, None, :]
    shifted, inverse, message, sent = tables(ids, child_leaf, edge_weights, child_pix, other_pix)
    near = home(ids, parent_pixels[:, None, :], child_pix, parent_leaf, message)
    pairs = [(cores * i, cores * j) for i, j in up] + [(cores * i + 1, cores * j + 1) for i, j in down]
    landed = lax.ppermute(after(sent, low, high, near), ("region", "batch"), pairs)
    child_flows, sums = flows(
        ids, child_pix, low, parent_flows, high, shifted, inverse, edge_weights
    )
    own_rows = states // cores
    outgoing = lax.dynamic_slice_in_dim(sums, (1 - core) * own_rows, own_rows, 2).astype(BF16)
    theirs = lax.ppermute(outgoing, "batch", swap)
    other = lax.ppermute(after(landed, theirs), "batch", swap)
    new_weights = update(ids, sums, theirs, inverse, shifted, edge_weights)
    parent_ll = gather(children, ids, landed, other, near)
    return parent_ll, child_flows, new_weights


def solution(mesh):
    return jax.shard_map(
        on_device,
        mesh=mesh,
        in_specs=(
            P("region", "batch"),
            P("region", "batch"),
            P("region", None, None),
            P("region", None, None),
            P("region", None, None),
            P(),
            P("region", "batch", None),
        ),
        out_specs=(
            P("region", "batch", None),
            P("region", "batch", None),
            P("region", "batch", None),
        ),
        check_vma=False,
    )
```

time: 139 us -> 73.1 us (0.53); the launches traced: 137 us -> 72.4 us
  Pallas kernels: 0 us -> 33.1 us
  other arithmetic: 28.7 us -> 1.34 us
  waiting for transfers between devices: 31.9 us -> 7.4 us
  local copies, waits for them, and re-layouts: 24.1 us -> 7.03 us
  matrix products: 16 us -> 0 us
  between operations: 14.3 us -> 0.71 us
    pallas_call x0 -> x7, Pallas kernels: none -> 33.1 us  [the longest x1 11.3 us: flows(): pl.pallas_call(flows_kernel, grid_spec=pltpu.PrefetchScalarGridSpec(num_s...]
    ppermute x4 -> x6, waiting for transfers between devices: 31.9 us -> 7.4 us  [the longest x1 5.61 us: on_device(): low = lax.ppermute(parent_flows, 'region', up)]
    gather x4 -> x0, local copies, waits for them, and re-layouts: 20.6 us -> none  [the longest x3 18.6 us: one_region(): return region_table[region_pixels]]
    dot_general x3 -> x0, matrix products: 16 us -> none  [the longest x1 7.26 us: on_device(): jnp.einsum('cbk,ckj->cbj', scaled, edge_weights, preferred_element_type=j...]
    convert_element_type x2 -> x0, other arithmetic: 7.46 us -> none  [the longest x1 4.51 us: on_device(): scaled = (upstream / totals).astype(jnp.bfloat16)]
    reduce_sum x3 -> x0, other arithmetic: 6.76 us -> none  [the longest x1 5.18 us: on_device(): jnp.sum(jnp.where((near_ids == position)[:, None, None], nearby, 0.0), ax...]
    div x1 -> x0, other arithmetic: 6.34 us -> none  [on_device(): states * counts / jnp.sum(counts, axis=-1, keepdims=True)]
    reduce_max x5 -> x0, other arithmetic: 4.09 us -> none  [the longest x1 2.45 us: on_device(): row_peak = jnp.max(loglik, axis=-1, keepdims=True)]
  transfers between devices with their start and end apart: 5 -> 6, of which waited for: 2 -> 3; matrix products, arithmetic and copies ran while one was open for 35% -> 8% of each run, Pallas kernels for 0% -> 38%
where the time goes in v1:
time: 73.1 us; the launch traced here: 72.4 us
  Pallas kernels  33.1 us (45%)
  starting transfers between devices  22.8 us (31%)
  waiting for transfers between devices  7.4 us (10%)
  local copies, waits for them, and re-layouts  7.03 us (10%)
  other arithmetic  1.34 us (2%)
    pallas_call x1, Pallas kernels, flows(): pl.pallas_call(flows_kernel, grid_spec=pltpu.PrefetchScalarGridSpec(num_s...  11.3 us
    ppermute x1, starting transfers between devices, on_device(): high = lax.ppermute(parent_flows, 'region', down)  8.62 us
    ppermute x1, starting transfers between devices, on_device(): lax.ppermute(after(sent, low, high, near), ('region', 'batch'), pairs)  8.21 us
    pallas_call x1, Pallas kernels, tables(): pl.pallas_call(tables_kernel, grid_spec=pltpu.PrefetchScalarGridSpec(num_...  6.73 us
    ppermute x1, waiting for transfers between devices, on_device(): low = lax.ppermute(parent_flows, 'region', up)  5.61 us
    pallas_call x1, Pallas kernels, gather(): pl.pallas_call(functools.partial(gather_kernel, children), grid_spec=pltp...  5.57 us
    pallas_call x1, Pallas kernels, update(): pl.pallas_call(update_kernel, grid_spec=pltpu.PrefetchScalarGridSpec(num_...  4.98 us
    pallas_call x1, Pallas kernels, home(): pl.pallas_call(home_kernel, grid_spec=pltpu.PrefetchScalarGridSpec(num_sc...  4.53 us
  transfers between devices with their start and end apart: 6, of which 3 were waited for; matrix products, arithmetic and copies ran while one was open for 8% of the time, Pallas kernels for 38%

profile of v1, /device:TPU:5, one launch (start us, length us, event | category | flops | bytes accessed | tf_op | source)
XLA Modules:
  0.0 72.4 jit_solution(3482162168272778774)
XLA Ops:
  0.6 3.2 %collective-permute-start.1 = (bf16[1,512,1024]{2,1,0:T(8,128)(2,1)}, bf16[1,512,1024]{2,1,0:T(8,128)(2,1)S(1)}, u32[]{:S(2)}, u32[]{:S(2)}) collective-permute-start(bf16[1,512,1024]{2,1,0:T(8,128)(2,1)} %here_ref.1), channel_id=1, source_target_pairs={{0,2},{2,4},{4,6},{6,8},{8,10},{10,12},{12,14},{14,16},{16,18},{18... | collective-permute-start | bytes 3145736 | tf_op jit(solution)/shard_map/ppermute | solution.py:289
  3.8 8.6 %collective-permute-start.2 = (bf16[1,512,1024]{2,1,0:T(8,128)(2,1)}, bf16[1,512,1024]{2,1,0:T(8,128)(2,1)S(1)}, u32[]{:S(2)}, u32[]{:S(2)}) collective-permute-start(bf16[1,512,1024]{2,1,0:T(8,128)(2,1)} %here_ref.1), channel_id=1, source_target_pairs={{2,0},{4,2},{6,4},{8,6},{10,8},{12,10},{14,12},{16,14},{18,16},{20... | collective-permute-start | bytes 3145736 | tf_op jit(solution)/shard_map/ppermute | solution.py:290
  12.5 1.0 %collective-permute-start = (s32[2,512]{1,0:T(2,128)}, s32[2,512]{1,0:T(2,128)S(1)}, u32[]{:S(2)}, u32[]{:S(2)}) collective-permute-start(s32[2,512]{1,0:T(2,128)} %param.7), channel_id=1, source_target_pairs={{0,1},{1,0},{2,3},{3,2},{4,5},{5,4},{6,7},{7,6},{8,9},{9,8},{10,11... | collective-permute-start | bytes 12296 | tf_op jit(solution)/shard_map/ppermute | solution.py:291
  13.5 1.3 %pad_add_fusion.ids_ref = s32[258]{0:T(512)} fusion(s32[1]{0:T(128)} %bitcast.1, s32[1]{0:T(128)} %bitcast, s32[256]{0:T(256)} %param.12), kind=kLoop, calls=%fused_computation.1 | loop fusion | flops 516 | bytes 2064 | tf_op jit(solution)/shard_map/concatenate | solution.py:287
  14.9 1.3 %broadcast_in_dim.9.mine_ref.child_pix_ref.pix_ref = s32[2,1,512]{2,1,0:T(1,128)} reshape(s32[2,512]{1,0:T(2,128)} %param.7) | data formatting | bytes 8192 | tf_op jit(solution)/shard_map/broadcast_in_dim | solution.py:288
  16.1 0.0 collective-permute-done
  16.1 0.6 broadcast_in_dim.10.theirs_ref
  16.7 6.7 %tables.1 = (bf16[2,256,1024]{2,1,0:T(8,128)(2,1)}, bf16[2,256,1024]{2,1,0:T(8,128)(2,1)}, bf16[2,256,1024]{2,1,0:T(8,128)(2,1)}, bf16[528,1024]{1,0:T(8,128)(2,1)}) custom-call(s32[258]{0:T(512)} %pad_add_fusion.ids_ref, bf16[2,1024,256]{2,1,0:T(8,128)(2,1)} %leaf_ref.2, bf16[2,1024,1024]{2,1,0:T(8,128)(2,1)} %weights_ref.5, ...), custom_call_target="tpu_custom_call" | custom-call | flops 1073741824 | bytes 12582912 | tf_op jit(solution)/shard_map/tables/pallas_call | solution.py:68
  23.5 4.5 %home.1.refs_3_.sofar_ref = f32[1,512,1024]{2,1,0:T(8,128)} custom-call(s32[258]{0:T(512)} %pad_add_fusion.ids_ref, s32[1,1,512]{2,1,0:T(1,128)} %bitcast.3, s32[2,1,512]{2,1,0:T(1,128)} %broadcast_in_dim.9.mine_ref.child_pix_ref.pix_ref, bf16[1,1024,256]{2,1,0:T(8,128)(2,1)} %leaf_ref.3, bf16[2,256,1024]{2,1,0:T(8,128)(2,1)} %get-tuple-element.10.message_ref), custom_call_target="tpu_custom_call" | custom-call | flops 805306368 | bytes 4194304 | tf_op jit(solution)/shard_map/home/pallas_call | solution.py:123
  28.0 5.6 %collective-permute-done.1.refs_1_.before_ref = bf16[1,512,1024]{2,1,0:T(8,128)(2,1)S(1)} collective-permute-done((bf16[1,512,1024]{2,1,0:T(8,128)(2,1)}, bf16[1,512,1024]{2,1,0:T(8,128)(2,1)S(1)}, u32[]{:S(2)}, u32[]{:S(2)}) %collective-permute-start.1) | collective-permute-done | bytes 1048608 | tf_op jit(solution)/shard_map/ppermute | solution.py:289
  33.6 0.0 copy-start.3
  33.6 1.0 %collective-permute-done.2.refs_2_.after_ref = bf16[1,512,1024]{2,1,0:T(8,128)(2,1)S(1)} collective-permute-done((bf16[1,512,1024]{2,1,0:T(8,128)(2,1)}, bf16[1,512,1024]{2,1,0:T(8,128)(2,1)S(1)}, u32[]{:S(2)}, u32[]{:S(2)}) %collective-permute-start.2) | collective-permute-done | bytes 1048608 | tf_op jit(solution)/shard_map/ppermute | solution.py:290
  34.6 0.0 copy-start.4
  34.6 0.0 copy-done.3
  34.6 1.0 %copy-done.4 = bf16[1,512,1024]{2,1,0:T(8,128)(2,1)} copy-done((bf16[1,512,1024]{2,1,0:T(8,128)(2,1)}, bf16[1,512,1024]{2,1,0:T(8,128)(2,1)S(1)}, u32[]{:S(2)}) %copy-start.4) | copy-done | bytes 1048600
  35.6 8.2 %collective-permute-start.3 = (bf16[528,1024]{1,0:T(8,128)(2,1)}, bf16[528,1024]{1,0:T(8,128)(2,1)S(1)}, u32[]{:S(2)}, u32[]{:S(2)}) collective-permute-start(bf16[528,1024]{1,0:T(8,128)(2,1)} %after.2), channel_id=1, source_target_pairs={{0,2},{2,4},{4,6},{6,8},{8,10},{10,12},{12,14},{14,16},{16,18},{18... | collective-permute-start | bytes 3244040 | tf_op jit(solution)/shard_map/ppermute | solution.py:295
  43.8 11.3 %flows.1 = (bf16[2,512,1024]{2,1,0:T(8,128)(2,1)}, f32[2,256,1024]{2,1,0:T(8,128)}) custom-call(s32[258]{0:T(512)} %pad_add_fusion.ids_ref, s32[2,1,512]{2,1,0:T(1,128)} %broadcast_in_dim.9.mine_ref.child_pix_ref.pix_ref, bf16[1,512,1024]{2,1,0:T(8,128)(2,1)} %copy-done.3, bf16[1,512,1024]{2,1,0:T(8,128)(2,1)} %here_ref.1, bf16[1,512,1024]{2,1,0:T(8,128)(2,1)} %copy-done.4, ...), custom_call_target="tpu_custom_call" | custom-call | flops 3758096384 | bytes 12582912 | tf_op jit(solution)/shard_map/flows/pallas_call | solution.py:173
  55.1 1.3 %dynamic-slice_convert_fusion = bf16[2,256,512]{2,1,0:T(8,128)(2,1)S(1)} fusion(f32[2,256,1024]{2,1,0:T(8,128)} %get-tuple-element.13.mine_ref, s32[]{:T(128)S(6)} %select_n.3), kind=kLoop, calls=%fused_computation | loop fusion | bytes 1048580 | tf_op jit(solution)/shard_map/convert_element_type | solution.py:300
  56.4 0.1 collective-permute-start.4
  56.5 0.0 collective-permute-done.3.landed_ref
  56.5 0.0 copy-start
  56.5 1.1 %copy.14.refs_0_ = bf16[528,1024]{1,0:T(8,128)(2,1)} copy(bf16[528,1024]{1,0:T(8,128)(2,1)S(1)} %collective-permute-done.3.landed_ref) | data formatting | bytes 2162688
  57.6 0.8 %collective-permute-done.4.refs_1_.theirs_ref = bf16[2,256,512]{2,1,0:T(8,128)(2,1)S(1)} collective-permute-done((bf16[2,256,512]{2,1,0:T(8,128)(2,1)S(1)}, bf16[2,256,512]{2,1,0:T(8,128)(2,1)S(1)}, u32[]{:S(2)}, u32[]{:S(2)}) %collective-permute-start.4) | collective-permute-done | bytes 524320 | tf_op jit(solution)/shard_map/ppermute | solution.py:301
  58.4 0.0 copy-start.1
  58.4 0.8 %copy-done.1 = bf16[2,256,512]{2,1,0:T(8,128)(2,1)} copy-done((bf16[2,256,512]{2,1,0:T(8,128)(2,1)}, bf16[2,256,512]{2,1,0:T(8,128)(2,1)S(1)}, u32[]{:S(2)}) %copy-start.1) | copy-done | bytes 524312
  59.2 0.0 copy-done
  59.2 1.6 %collective-permute-start.5 = (bf16[528,1024]{1,0:T(8,128)(2,1)}, bf16[528,1024]{1,0:T(8,128)(2,1)S(1)}, u32[]{:S(2)}, u32[]{:S(2)}) collective-permute-start(bf16[528,1024]{1,0:T(8,128)(2,1)} %after.3), channel_id=1, source_target_pairs={{0,1},{1,0},{2,3},{3,2},{4,5},{5,4},{6,7},{7,6},{8,9},{9,8},{10,11... | collective-permute-start | bytes 3244040 | tf_op jit(solution)/shard_map/ppermute | solution.py:302
  60.8 5.0 %update.1 = bf16[2,512,1024]{2,1,0:T(8,128)(2,1)} custom-call(s32[258]{0:T(512)} %pad_add_fusion.ids_ref, f32[2,256,1024]{2,1,0:T(8,128)} %get-tuple-element.13.mine_ref, bf16[2,256,512]{2,1,0:T(8,128)(2,1)} %copy-done.1, bf16[2,256,1024]{2,1,0:T(8,128)(2,1)} %get-tuple-element.12.inverse_ref, bf16[2,256,1024]{2,1,0:T(8,128)(2,1)} %get-tuple-element.11.shifted_ref, ...), custom_call_target="tpu_custom_call" | custom-call | flops 536870912 | bytes 8388608 | tf_op jit(solution)/shard_map/update/pallas_call | solution.py:216
  65.8 0.0 collective-permute-done.5.other_ref
  65.8 0.0 copy-start.2
  65.8 1.0 %copy-done.2 = bf16[528,1024]{1,0:T(8,128)(2,1)} copy-done((bf16[528,1024]{1,0:T(8,128)(2,1)}, bf16[528,1024]{1,0:T(8,128)(2,1)S(1)}, u32[]{:S(2)}) %copy-start.2) | copy-done | bytes 1081368
  66.8 5.6 %gather.1 = f32[1,512,1024]{2,1,0:T(8,128)} custom-call(s32[258]{0:T(512)} %pad_add_fusion.ids_ref, bf16[528,1024]{1,0:T(8,128)(2,1)} %copy-done, bf16[528,1024]{1,0:T(8,128)(2,1)} %copy-done.2, f32[1,512,1024]{2,1,0:T(8,128)} %home.1.refs_3_.sofar_ref), custom_call_target="tpu_custom_call", output_to_operand_aliasing={{}: (3, {})} | custom-call | flops 553648128 | bytes 6291456 | tf_op jit(solution)/shard_map/gather/pallas_call | solution.py:261
  (2 shorter events, 0.0 us)
Async XLA Ops:
  0.6 33.0 %collective-permute-start.1 = (bf16[1,512,1024]{2,1,0:T(8,128)(2,1)}, bf16[1,512,1024]{2,1,0:T(8,128)(2,1)S(1)}, u32[]{:S(2)}, u32[]{:S(2)}) collective-permute-start(bf16[1,512,1024]{2,1,0:T(8,128)(2,1)} %here_ref.1), channel_id=1, source_target_pairs={{0,2},{2,4},{4,6},{6,8},{8,10},{10,12},{12,14},{14,16},{16,18},{18... | collective-permute-start | bytes 3145736 | tf_op jit(solution)/shard_map/ppermute | solution.py:289
  3.8 30.8 %collective-permute-start.2 = (bf16[1,512,1024]{2,1,0:T(8,128)(2,1)}, bf16[1,512,1024]{2,1,0:T(8,128)(2,1)S(1)}, u32[]{:S(2)}, u32[]{:S(2)}) collective-permute-start(bf16[1,512,1024]{2,1,0:T(8,128)(2,1)} %here_ref.1), channel_id=1, source_target_pairs={{2,0},{4,2},{6,4},{8,6},{10,8},{12,10},{14,12},{16,14},{18,16},{20... | collective-permute-start | bytes 3145736 | tf_op jit(solution)/shard_map/ppermute | solution.py:290
  12.5 3.7 %collective-permute-start = (s32[2,512]{1,0:T(2,128)}, s32[2,512]{1,0:T(2,128)S(1)}, u32[]{:S(2)}, u32[]{:S(2)}) collective-permute-start(s32[2,512]{1,0:T(2,128)} %param.7), channel_id=1, source_target_pairs={{0,1},{1,0},{2,3},{3,2},{4,5},{5,4},{6,7},{7,6},{8,9},{9,8},{10,11... | collective-permute-start | bytes 12296 | tf_op jit(solution)/shard_map/ppermute | solution.py:291
  33.6 1.0 %copy-start.3 = (bf16[1,512,1024]{2,1,0:T(8,128)(2,1)}, bf16[1,512,1024]{2,1,0:T(8,128)(2,1)S(1)}, u32[]{:S(2)}) copy-start(bf16[1,512,1024]{2,1,0:T(8,128)(2,1)S(1)} %collective-permute-done.1.refs_1_.before_ref) | copy-start | bytes 3145732
  34.6 1.0 %copy-start.4 = (bf16[1,512,1024]{2,1,0:T(8,128)(2,1)}, bf16[1,512,1024]{2,1,0:T(8,128)(2,1)S(1)}, u32[]{:S(2)}) copy-start(bf16[1,512,1024]{2,1,0:T(8,128)(2,1)S(1)} %collective-permute-done.2.refs_2_.after_ref) | copy-start | bytes 3145732
  35.6 20.9 %collective-permute-start.3 = (bf16[528,1024]{1,0:T(8,128)(2,1)}, bf16[528,1024]{1,0:T(8,128)(2,1)S(1)}, u32[]{:S(2)}, u32[]{:S(2)}) collective-permute-start(bf16[528,1024]{1,0:T(8,128)(2,1)} %after.2), channel_id=1, source_target_pairs={{0,2},{2,4},{4,6},{6,8},{8,10},{10,12},{12,14},{14,16},{16,18},{18... | collective-permute-start | bytes 3244040 | tf_op jit(solution)/shard_map/ppermute | solution.py:295
  56.4 2.0 %collective-permute-start.4 = (bf16[2,256,512]{2,1,0:T(8,128)(2,1)S(1)}, bf16[2,256,512]{2,1,0:T(8,128)(2,1)S(1)}, u32[]{:S(2)}, u32[]{:S(2)}) collective-permute-start(bf16[2,256,512]{2,1,0:T(8,128)(2,1)S(1)} %dynamic-slice_convert_fusion), channel_id=1, source_target_pairs={{0,1},{1,0},{2,3},{3,2},{4,5},{5,4},{6,7},{7,6},{8,9},{9,8},{10,11... | collective-permute-start | bytes 1572872 | tf_op jit(solution)/shard_map/ppermute | solution.py:301
  56.5 2.7 %copy-start = (bf16[528,1024]{1,0:T(8,128)(2,1)}, bf16[528,1024]{1,0:T(8,128)(2,1)S(1)}, u32[]{:S(2)}) copy-start(bf16[528,1024]{1,0:T(8,128)(2,1)S(1)} %collective-permute-done.3.landed_ref) | copy-start | bytes 3244036
  58.4 0.8 %copy-start.1 = (bf16[2,256,512]{2,1,0:T(8,128)(2,1)}, bf16[2,256,512]{2,1,0:T(8,128)(2,1)S(1)}, u32[]{:S(2)}) copy-start(bf16[2,256,512]{2,1,0:T(8,128)(2,1)S(1)} %collective-permute-done.4.refs_1_.theirs_ref) | copy-start | bytes 1572868
  59.2 6.6 %collective-permute-start.5 = (bf16[528,1024]{1,0:T(8,128)(2,1)}, bf16[528,1024]{1,0:T(8,128)(2,1)S(1)}, u32[]{:S(2)}, u32[]{:S(2)}) collective-permute-start(bf16[528,1024]{1,0:T(8,128)(2,1)} %after.3), channel_id=1, source_target_pairs={{0,1},{1,0},{2,3},{3,2},{4,5},{5,4},{6,7},{7,6},{8,9},{9,8},{10,11... | collective-permute-start | bytes 3244040 | tf_op jit(solution)/shard_map/ppermute | solution.py:302
  65.8 1.0 %copy-start.2 = (bf16[528,1024]{1,0:T(8,128)(2,1)}, bf16[528,1024]{1,0:T(8,128)(2,1)S(1)}, u32[]{:S(2)}) copy-start(bf16[528,1024]{1,0:T(8,128)(2,1)S(1)} %collective-permute-done.5.other_ref) | copy-start | bytes 3244036

commit v2 on v0

v2 whole, which is shorter than its diff:
```python
import functools

import jax
import jax.numpy as jnp
from jax import lax
from jax.experimental import pallas as pl
from jax.experimental.pallas import tpu as pltpu
from jax.sharding import PartitionSpec as P

PRIOR = 0.05
F32, BF16 = jnp.float32, jnp.bfloat16
MIB = 2**20


def log_softmax_by_value(leaf):
    logits = jnp.transpose(leaf.astype(F32))
    top = jnp.max(logits, axis=0, keepdims=True)
    logits = logits - top
    return logits - jnp.log(jnp.sum(jnp.exp(logits), axis=0, keepdims=True))


def one_hot_rows(pixels, values):
    rows = lax.broadcasted_iota(jnp.int32, (values, pixels.shape[1]), 0)
    return jnp.where(rows == pixels, 1.0, 0.0).astype(F32)


def one_hot(pixels, values):
    count = pixels.shape[1]
    column = jnp.transpose(jnp.broadcast_to(pixels.astype(F32), (8, count)))[:, :1]
    columns = lax.broadcasted_iota(jnp.int32, (count, values), 1).astype(F32)
    return jnp.where(columns == column, 1.0, 0.0).astype(BF16)


def dot(a, b):
    return jnp.dot(a, b, preferred_element_type=F32)


def dot_t(a, b):
    return lax.dot_general(a, b, (((1,), (1,)), ((), ())), preferred_element_type=F32)


def call(kernel, name, grid, in_specs, out_specs, out_shape, args, flops, scalars=1, vmem=26, **more):
    return pl.pallas_call(
        kernel,
        grid_spec=pltpu.PrefetchScalarGridSpec(
            num_scalar_prefetch=scalars,
            grid=grid,
            in_specs=in_specs,
            out_specs=out_specs,
            scratch_shapes=more.pop("scratch", ()),
        ),
        out_shape=out_shape,
        compiler_params=pltpu.CompilerParams(vmem_limit_bytes=vmem * MIB),
        cost_estimate=pl.CostEstimate(flops=flops // 10**6, bytes_accessed=8, transcendentals=0),
        name=name,
        **more,
    )(*args)


def shape(*dims, dtype=BF16):
    return jax.ShapeDtypeStruct(dims, dtype)


TOKEN = shape(8, 128, dtype=F32)


def whole(array):
    return pl.BlockSpec(array.shape, lambda *_: (0,) * array.ndim)


def after(value, *others):
    anywhere = pl.BlockSpec(memory_space=pl.ANY)
    return pl.pallas_call(
        lambda *refs: None,
        in_specs=[anywhere] * (1 + len(others)),
        out_specs=anywhere,
        out_shape=jax.ShapeDtypeStruct(value.shape, value.dtype),
        input_output_aliases={0: 0},
        compiler_params=pltpu.CompilerParams(vmem_limit_bytes=MIB),
        cost_estimate=pl.CostEstimate(flops=0, bytes_accessed=0, transcendentals=0),
        name="after",
    )(value, *others)


def tables_kernel(
    leaf_ref, weights_ref, mine_ref, theirs_ref, shifted_ref, inverse_ref, message_ref, sent_ref
):
    child = pl.program_id(0)
    table = log_softmax_by_value(leaf_ref[0])
    peak = jnp.max(table, axis=1, keepdims=True)
    shifted = jnp.exp(table - peak).astype(BF16)
    shifted_ref[0] = shifted
    totals = dot_t(shifted, weights_ref[0])
    inverse_ref[0] = (1.0 / totals).astype(BF16)
    message = (peak + jnp.log(totals)).astype(BF16)
    message_ref[0] = message
    values = message.shape[0]
    sent_ref[pl.ds(pl.multiple_of(child * values, values), values)] = message

    @pl.when(child == 0)
    def _():
        children = mine_ref.shape[0]
        own = jnp.concatenate([mine_ref[c : c + 1] for c in range(children)], axis=1)
        other = jnp.concatenate([theirs_ref[c : c + 1] for c in range(children)], axis=1)
        half = lax.broadcasted_iota(jnp.int32, (16, own.shape[1]), 0)
        rows = jnp.where(half == lax.axis_index("batch"), own, other)
        sent_ref[sent_ref.shape[0] - 16 :] = rows.astype(F32).astype(BF16)


def tables(leaf, weights, mine, theirs):
    children, states, values = leaf.shape
    one = lambda *block: pl.BlockSpec((1, *block), lambda c: (c, 0, 0))
    sent = shape(children * values + 16, states)
    return call(
        tables_kernel, "tables", (children,),
        [one(states, values), one(states, states), whole(mine), whole(theirs)],
        [one(values, states)] * 3 + [whole(sent)],
        [shape(children, values, states)] * 3 + [sent],
        (leaf, weights, mine, theirs),
        2 * children * values * states**2,
        scalars=0,
    )


def rows_kernel(
    ids_ref, parent_pix_ref, pix_ref, leaf_ref, message_ref, shifted_ref, inverse_ref,
    shifted_rows_ref, inverse_rows_ref, out_ref, token_ref,
):
    token_ref[...] = jnp.zeros_like(token_ref)
    child, children = pl.program_id(0), pix_ref.shape[0]
    position = lax.axis_index("region")
    values = message_ref.shape[1]
    hot = one_hot(pix_ref[pl.ds(child, 1)], values)
    shifted_rows_ref[0] = dot(hot, shifted_ref[0]).astype(BF16)
    inverse_rows_ref[0] = dot(hot, inverse_ref[0]).astype(BF16)
    mine = jnp.where(ids_ref[position * children + child] == position, 1.0, 0.0)
    message = dot(hot, message_ref[0]) * mine

    @pl.when(child == 0)
    def _():
        logits = leaf_ref[0]
        wide = logits.astype(F32)
        top = jnp.max(wide, axis=1, keepdims=True)
        norm = top + jnp.log(jnp.sum(jnp.exp(wide - top), axis=1, keepdims=True))
        norm_row = jnp.transpose(jnp.broadcast_to(norm, (norm.shape[0], 128)))[:1]
        parent_hot = one_hot(parent_pix_ref[...], values)
        out_ref[0] = dot_t(parent_hot, logits) - norm_row + message

    @pl.when(child > 0)
    def _():
        out_ref[0] += message


def rows(ids, parent_pix, pix, leaf, message, shifted, inverse):
    children, values, states = message.shape
    samples = pix.shape[1]
    one = lambda *block: pl.BlockSpec((1, *block), lambda c, ids: (c, 0, 0))
    out = shape(1, samples, states, dtype=F32)
    return call(
        rows_kernel, "rows", (children,),
        [whole(parent_pix), whole(pix), whole(leaf)] + [one(values, states)] * 3,
        [one(samples, states)] * 2 + [whole(out), whole(TOKEN)],
        [shape(children, samples, states)] * 2 + [out, TOKEN],
        (ids, parent_pix, pix, leaf, message, shifted, inverse),
        2 * samples * states * values * (3 * children + 1),
    )


def flows_kernel(
    ids_ref, pix_ref, before_ref, here_ref, after_ref, shifted_ref, inverse_ref, weights_ref,
    flows_ref, mine_ref, theirs_ref,
):
    child, children = pl.program_id(0), pl.num_programs(0)
    position, core = lax.axis_index("region"), lax.axis_index("batch")
    source = ids_ref[position * children + child] - position
    above = jnp.where(
        source == 0, here_ref[0], jnp.where(source < 0, before_ref[0], after_ref[0])
    )
    scaled = (above.astype(F32) * inverse_ref[0].astype(F32)).astype(BF16)
    pulled = dot(scaled, weights_ref[0])
    flows_ref[0] = (shifted_ref[0].astype(F32) * pulled).astype(BF16)
    values, part = mine_ref.shape[1:]
    hot_rows = one_hot_rows(pix_ref[pl.ds(child, 1)], values).astype(BF16)
    sums = dot(hot_rows, above)
    low, high = sums[:, :part], sums[:, part:]
    mine_ref[0] = jnp.where(core == 0, low, high)
    theirs_ref[0] = jnp.where(core == 0, high, low).astype(BF16)


def flows(ids, pix, before, here, after, shifted, inverse, weights, values):
    children, samples, states = shifted.shape
    one = lambda *block: pl.BlockSpec((1, *block), lambda c, ids: (c, 0, 0))
    return call(
        flows_kernel, "flows", (children,),
        [whole(pix), whole(before), whole(here), whole(after)]
        + [one(samples, states)] * 2 + [one(states, states)],
        [one(samples, states), one(values, states // 2), one(values, states // 2)],
        [
            shape(children, samples, states),
            shape(children, values, states // 2, dtype=F32),
            shape(children, values, states // 2),
        ],
        (ids, pix, before, here, after, shifted, inverse, weights),
        5 * 10**16,
        vmem=26,
    )


def update_kernel(
    mine_ref, theirs_ref, inverse_ref, shifted_ref, weights_ref, out_ref, token_ref, held_ref, sems
):
    child, step = pl.program_id(0), pl.program_id(1)
    children, count, _ = held_ref.shape
    width = out_ref.shape[1]
    start = pl.multiple_of(lax.axis_index("batch") * count, count)
    token_ref[...] = jnp.zeros_like(token_ref)

    def fetch(c):
        return pltpu.make_async_copy(
            weights_ref.at[c, pl.ds(start, count)], held_ref.at[c], sems.at[c]
        )

    @pl.when(jnp.logical_and(child == 0, step == 0))
    def _():
        for c in range(children):
            fetch(c).start()

    here = pl.multiple_of(step * width, width)
    inverse = inverse_ref[0, :, pl.ds(pl.multiple_of(start + here, width), width)]
    sums = (mine_ref[0] + theirs_ref[0].astype(F32)) * inverse.astype(F32)
    pairs = dot(jnp.transpose(sums).astype(BF16), shifted_ref[0])

    @pl.when(step == 0)
    def _():
        fetch(child).wait()

    counts = held_ref[child, pl.ds(here, width)].astype(F32) * pairs + PRIOR
    scale = counts.shape[1] / jnp.sum(counts, axis=1, keepdims=True)
    out_ref[0] = (counts * scale).astype(BF16)


def update(mine, theirs, inverse, shifted, weights):
    children, values, states = shifted.shape
    count = mine.shape[2]
    steps = 2
    width = count // steps
    block = pl.BlockSpec((1, values, width), lambda c, i: (c, 0, i))
    table = pl.BlockSpec((1, values, states), lambda c, i: (c, 0, 0))
    return call(
        update_kernel, "update", (children, steps),
        [block, block, table, table, pl.BlockSpec(memory_space=pltpu.HBM)],
        [pl.BlockSpec((1, width, states), lambda c, i: (c, i, 0)), whole(TOKEN)],
        [shape(children, count, states), TOKEN],
        (mine, theirs, inverse, shifted, weights),
        2 * children * count * states * values,
        vmem=26,
        scalars=0,
        scratch=[pltpu.VMEM((children, count, states), BF16), pltpu.SemaphoreType.DMA((children,))],
    )


def gather_kernel(children, landed, ids_ref, table_ref, pix_ref, sofar_ref, out_ref, hot_ref):
    count = ids_ref.shape[0]
    position, core = lax.axis_index("region"), lax.axis_index("batch")
    samples = out_ref.shape[1]
    values = table_ref.shape[0] // children
    neighbour = jnp.where((core == 0) == landed, position - 1, position + 1)
    out_ref[...] = sofar_ref[...]
    for c in range(children):
        child = neighbour * children + c
        there = jnp.logical_and(child >= 0, child < count)
        parent = ids_ref[jnp.clip(child, 0, count - 1)]

        @pl.when(jnp.logical_and(there, parent == position))
        def _():
            @pl.when(pl.program_id(0) == 0)
            def _():
                halves = pix_ref[...].astype(F32)
                pixels = jnp.where(core == 0, halves[0:1], halves[1:2])
                hot_ref[c] = one_hot(pixels[:, c * samples : (c + 1) * samples], values)

            out_ref[0] += dot(hot_ref[c], table_ref[c * values : (c + 1) * values])


def gather(children, landed, ids, tables, sofar):
    samples, states = sofar.shape[1:]
    span = tables.shape[0] - 16
    steps = 4
    width = states // steps
    out = pl.BlockSpec((1, samples, width), lambda i, ids: (0, 0, i))
    return call(
        functools.partial(gather_kernel, children, landed), "landed" if landed else "other", (steps,),
        [
            pl.BlockSpec((span, width), lambda i, ids: (0, i)),
            pl.BlockSpec((16, states), lambda i, ids: (span // 16, 0)),
            out,
        ],
        out, shape(*sofar.shape, dtype=F32),
        (ids, tables, tables, sofar),
        2 * samples * span * states,
        vmem=20,
        scratch=[pltpu.VMEM((children, samples, span // children), BF16)],
    )


def on_device(
    child_pixels, parent_pixels, child_leaf, parent_leaf, edge_weights, parent_of, parent_flows
):
    regions, cores = lax.axis_size("region"), lax.axis_size("batch")
    up = [(i, i + 1) for i in range(regions - 1)]
    down = [(i + 1, i) for i in range(regions - 1)]
    swap = [(0, 1), (1, 0)]
    children, values = child_pixels.shape[0], child_leaf.shape[2]

    low = lax.ppermute(parent_flows, "region", up)
    high = lax.ppermute(parent_flows, "region", down)
    other_pix = lax.ppermute(child_pixels, "batch", swap)
    shifted, inverse, message, sent = tables(child_leaf, edge_weights, child_pixels, other_pix)
    shifted_rows, inverse_rows, near, looked_up = rows(
        parent_of, parent_pixels, child_pixels, parent_leaf, message, shifted, inverse
    )
    pairs = [(cores * i, cores * j) for i, j in up] + [(cores * i + 1, cores * j + 1) for i, j in down]
    landed = lax.ppermute(after(sent, looked_up), ("region", "batch"), pairs)
    child_flows, mine, theirs = flows(
        parent_of, child_pixels, low, parent_flows, high, shifted_rows, inverse_rows, edge_weights, values
    )
    theirs = lax.ppermute(theirs, "batch", swap)
    new_weights, updated = update(mine, theirs, inverse, shifted, edge_weights)
    landed = after(landed, updated)
    other = lax.ppermute(landed, "batch", swap)
    near = gather(children, True, parent_of, landed, near)
    parent_ll = gather(children, False, parent_of, other, near)
    return parent_ll, child_flows, new_weights


def solution(mesh):
    return jax.shard_map(
        on_device,
        mesh=mesh,
        in_specs=(
            P("region", "batch"),
            P("region", "batch"),
            P("region", None, None),
            P("region", None, None),
            P("region", None, None),
            P(),
            P("region", "batch", None),
        ),
        out_specs=(
            P("region", "batch", None),
            P("region", "batch", None),
            P("region", "batch", None),
        ),
        check_vma=False,
    )
```

time: 139 us -> 54.6 us (0.39); the launches traced: 137 us -> 53.6 us
  other arithmetic: 28.7 us -> 0 us
  waiting for transfers between devices: 31.9 us -> 7.48 us
  Pallas kernels: 0 us -> 21.6 us
  local copies, waits for them, and re-layouts: 24.1 us -> 4.13 us
  matrix products: 16 us -> 0 us
  between operations: 14.3 us -> 0.76 us
  starting transfers between devices: 21.7 us -> 19.6 us
    ppermute x4 -> x6, waiting for transfers between devices: 31.9 us -> 7.48 us  [the longest x1 3.9 us: on_device(): low = lax.ppermute(parent_flows, 'region', up)]
    pallas_call x0 -> x8, Pallas kernels: none -> 21.6 us  [the longest x6 21.6 us: call(): pl.pallas_call(kernel, grid_spec=pltpu.PrefetchScalarGridSpec(num_scalar_...]
    gather x4 -> x0, local copies, waits for them, and re-layouts: 20.6 us -> none  [the longest x3 18.6 us: one_region(): return region_table[region_pixels]]
    dot_general x3 -> x0, matrix products: 16 us -> none  [the longest x1 7.26 us: on_device(): jnp.einsum('cbk,ckj->cbj', scaled, edge_weights, preferred_element_type=j...]
    convert_element_type x2 -> x0, other arithmetic: 7.46 us -> none  [the longest x1 4.51 us: on_device(): scaled = (upstream / totals).astype(jnp.bfloat16)]
    reduce_sum x3 -> x0, other arithmetic: 6.76 us -> none  [the longest x1 5.18 us: on_device(): jnp.sum(jnp.where((near_ids == position)[:, None, None], nearby, 0.0), ax...]
    div x1 -> x0, other arithmetic: 6.34 us -> none  [on_device(): states * counts / jnp.sum(counts, axis=-1, keepdims=True)]
    reduce_max x5 -> x0, other arithmetic: 4.09 us -> none  [the longest x1 2.45 us: on_device(): row_peak = jnp.max(loglik, axis=-1, keepdims=True)]
  transfers between devices with their start and end apart: 5 -> 6, of which waited for: 2 -> 4; matrix products, arithmetic and copies ran while one was open for 35% -> 0% of each run, Pallas kernels for 0% -> 34%
where the time goes in v2:
time: 54.6 us; the launch traced here: 53.6 us
  Pallas kernels  21.6 us (40%)
  starting transfers between devices  19.6 us (36%)
  waiting for transfers between devices  7.48 us (14%)
  local copies, waits for them, and re-layouts  4.13 us (8%)
  between operations  0.76 us (1%)
    pallas_call x6, Pallas kernels, call(): pl.pallas_call(kernel, grid_spec=pltpu.PrefetchScalarGridSpec(num_scalar_...  21.6 us
    ppermute x1, starting transfers between devices, on_device(): high = lax.ppermute(parent_flows, 'region', down)  8.62 us
    unnamed x18, local copies, waits for them, and re-layouts  4.13 us
    ppermute x1, waiting for transfers between devices, on_device(): low = lax.ppermute(parent_flows, 'region', up)  3.9 us
    ppermute x1, starting transfers between devices, on_device(): landed = lax.ppermute(after(sent, looked_up), ('region', 'batch'), pairs)  3.63 us
    ppermute x1, starting transfers between devices, on_device(): low = lax.ppermute(parent_flows, 'region', up)  3.21 us
    ppermute x1, starting transfers between devices, on_device(): theirs = lax.ppermute(theirs, 'batch', swap)  2.69 us
    ppermute x1, waiting for transfers between devices, on_device(): theirs = lax.ppermute(theirs, 'batch', swap)  1.54 us
  transfers between devices with their start and end apart: 6, of which 4 were waited for; matrix products, arithmetic and copies ran while one was open for 0% of the time, Pallas kernels for 34%

profile of v2, /device:TPU:5, one launch (start us, length us, event | category | flops | bytes accessed | tf_op | source)
XLA Modules:
  0.0 53.6 jit_solution(507307379382726367)
XLA Ops:
  0.6 3.2 %collective-permute-start.2 = (bf16[1,512,1024]{2,1,0:T(8,128)(2,1)}, bf16[1,512,1024]{2,1,0:T(8,128)(2,1)S(1)}, u32[]{:S(2)}, u32[]{:S(2)}) collective-permute-start(bf16[1,512,1024]{2,1,0:T(8,128)(2,1)} %here_ref.1), channel_id=1, source_target_pairs={{0,2},{2,4},{4,6},{6,8},{8,10},{10,12},{12,14},{14,16},{16,18},{18... | collective-permute-start | bytes 3145736 | tf_op jit(solution)/shard_map/ppermute | solution.py:315
  3.8 8.6 %collective-permute-start.3 = (bf16[1,512,1024]{2,1,0:T(8,128)(2,1)}, bf16[1,512,1024]{2,1,0:T(8,128)(2,1)S(1)}, u32[]{:S(2)}, u32[]{:S(2)}) collective-permute-start(bf16[1,512,1024]{2,1,0:T(8,128)(2,1)} %here_ref.1), channel_id=1, source_target_pairs={{2,0},{4,2},{6,4},{8,6},{10,8},{12,10},{14,12},{16,14},{18,16},{20... | collective-permute-start | bytes 3145736 | tf_op jit(solution)/shard_map/ppermute | solution.py:316
  12.5 1.0 %collective-permute-start = (s32[2,512]{1,0:T(2,128)}, s32[2,512]{1,0:T(2,128)S(1)}, u32[]{:S(2)}, u32[]{:S(2)}) collective-permute-start(s32[2,512]{1,0:T(2,128)} %pix_ref.3), channel_id=1, source_target_pairs={{0,1},{1,0},{2,3},{3,2},{4,5},{5,4},{6,7},{7,6},{8,9},{9,8},{10,11... | collective-permute-start | bytes 12296 | tf_op jit(solution)/shard_map/ppermute | solution.py:317
  13.5 1.0 %collective-permute-done.theirs_ref = s32[2,512]{1,0:T(2,128)S(1)} collective-permute-done((s32[2,512]{1,0:T(2,128)}, s32[2,512]{1,0:T(2,128)S(1)}, u32[]{:S(2)}, u32[]{:S(2)}) %collective-permute-start) | collective-permute-done | bytes 4128 | tf_op jit(solution)/shard_map/ppermute | solution.py:317
  14.6 2.2 %copy-done = bf16[2,1024,1024]{2,1,0:T(8,128)(2,1)S(1)} copy-done((bf16[2,1024,1024]{2,1,0:T(8,128)(2,1)S(1)}, bf16[2,1024,1024]{2,1,0:T(8,128)(2,1)}, u32[]{:S(2)}) %copy-start) | copy-done | bytes 4194328
  16.7 0.0 copy-start.2
  16.7 1.2 %copy-done.2 = bf16[2,1024,256]{2,1,0:T(8,128)(2,1)S(1)} copy-done((bf16[2,1024,256]{2,1,0:T(8,128)(2,1)S(1)}, bf16[2,1024,256]{2,1,0:T(8,128)(2,1)}, u32[]{:S(2)}) %copy-start.2) | copy-done | bytes 1048600
  18.0 0.0 copy-start.4
  18.0 0.7 %copy-done.4 = s32[2,512]{1,0:T(2,128)S(1)} copy-done((s32[2,512]{1,0:T(2,128)S(1)}, s32[2,512]{1,0:T(2,128)}, u32[]{:S(2)}) %copy-start.4) | copy-done | bytes 4120
  18.7 0.0 copy-start.3
  18.7 2.8 %tables.1 = (bf16[2,256,1024]{2,1,0:T(8,128)(2,1)S(1)}, bf16[2,256,1024]{2,1,0:T(8,128)(2,1)S(1)}, bf16[2,256,1024]{2,1,0:T(8,128)(2,1)S(1)}, bf16[528,1024]{1,0:T(8,128)(2,1)S(1)}) custom-call(bf16[2,1024,256]{2,1,0:T(8,128)(2,1)S(1)} %copy-done.2, bf16[2,1024,1024]{2,1,0:T(8,128)(2,1)S(1)} %copy-done, s32[2,512]{1,0:T(2,128)S(1)} %copy-done.4, ...), custom_call_target="tpu_custom_call" | custom-call | flops 1073 | bytes 8 | tf_op jit(solution)/shard_map/tables/pallas_call | solution.py:43
  21.5 0.0 copy-done.3
  21.5 0.0 copy-done.5
  21.5 0.0 copy-done.6
  21.5 0.0 copy-done.7
  21.5 0.0 copy-start.1
  21.5 0.0 copy-start.8
  21.5 4.6 %rows.1 = (bf16[2,512,1024]{2,1,0:T(8,128)(2,1)S(1)}, bf16[2,512,1024]{2,1,0:T(8,128)(2,1)S(1)}, f32[1,512,1024]{2,1,0:T(8,128)S(1)}, f32[8,128]{1,0:T(8,128)S(1)}) custom-call(s32[256]{0:T(256)S(1)} %copy-done.6, s32[1,512]{1,0:T(1,128)S(1)} %copy-done.7, s32[2,512]{1,0:T(2,128)S(1)} %copy-done.5, bf16[1,1024,256]{2,1,0:T(8,128)(2,1)S(1)} %copy-done.3, ...), custom_call_target="tpu_custom_call" | custom-call | flops 1879 | bytes 8 | tf_op jit(solution)/shard_map/rows/pallas_call | solution.py:43
  26.1 3.6 %collective-permute-start.1 = (bf16[528,1024]{1,0:T(8,128)(2,1)S(1)}, bf16[528,1024]{1,0:T(8,128)(2,1)S(1)}, u32[]{:S(2)}, u32[]{:S(2)}) collective-permute-start(bf16[528,1024]{1,0:T(8,128)(2,1)S(1)} %after.2), channel_id=1, source_target_pairs={{0,2},{2,4},{4,6},{6,8},{8,10},{10,12},{12,14},{14,16},{16,18},{18... | collective-permute-start | bytes 3244040 | tf_op jit(solution)/shard_map/ppermute | solution.py:323
  29.7 3.9 %collective-permute-done.2.before_ref = bf16[1,512,1024]{2,1,0:T(8,128)(2,1)S(1)} collective-permute-done((bf16[1,512,1024]{2,1,0:T(8,128)(2,1)}, bf16[1,512,1024]{2,1,0:T(8,128)(2,1)S(1)}, u32[]{:S(2)}, u32[]{:S(2)}) %collective-permute-start.2) | collective-permute-done | bytes 1048608 | tf_op jit(solution)/shard_map/ppermute | solution.py:315
  33.6 1.0 %collective-permute-done.3.after_ref = bf16[1,512,1024]{2,1,0:T(8,128)(2,1)S(1)} collective-permute-done((bf16[1,512,1024]{2,1,0:T(8,128)(2,1)}, bf16[1,512,1024]{2,1,0:T(8,128)(2,1)S(1)}, u32[]{:S(2)}, u32[]{:S(2)}) %collective-permute-start.3) | collective-permute-done | bytes 1048608 | tf_op jit(solution)/shard_map/ppermute | solution.py:316
  34.6 0.0 copy-done.1
  34.6 0.0 copy-done.8
  34.6 4.6 %flows.1 = (bf16[2,512,1024]{2,1,0:T(8,128)(2,1)}, f32[2,256,512]{2,1,0:T(8,128)S(1)}, bf16[2,256,512]{2,1,0:T(8,128)(2,1)S(1)}) custom-call(s32[256]{0:T(256)S(1)} %copy-done.6, s32[2,512]{1,0:T(2,128)S(1)} %copy-done.5, bf16[1,512,1024]{2,1,0:T(8,128)(2,1)S(1)} %collective-permute-done.2.before_ref, bf16[1,512,1024]{2,1,0:T(8,128)(2,1)S(1)} %copy-done.8, ...), custom_call_target="tpu_custom_call" | custom-call | flops 49999998976 | bytes 8 | tf_op jit(solution)/shard_map/flows/pallas_call | solution.py:43
  39.2 2.7 %collective-permute-start.4 = (bf16[2,256,512]{2,1,0:T(8,128)(2,1)S(1)}, bf16[2,256,512]{2,1,0:T(8,128)(2,1)S(1)}, u32[]{:S(2)}, u32[]{:S(2)}) collective-permute-start(bf16[2,256,512]{2,1,0:T(8,128)(2,1)S(1)} %get-tuple-element.24), channel_id=1, source_target_pairs={{0,1},{1,0},{2,3},{3,2},{4,5},{5,4},{6,7},{7,6},{8,9},{9,8},{10,11... | collective-permute-start | bytes 1572872 | tf_op jit(solution)/shard_map/ppermute | solution.py:327
  41.9 1.5 %collective-permute-done.4.theirs_ref = bf16[2,256,512]{2,1,0:T(8,128)(2,1)S(1)} collective-permute-done((bf16[2,256,512]{2,1,0:T(8,128)(2,1)S(1)}, bf16[2,256,512]{2,1,0:T(8,128)(2,1)S(1)}, u32[]{:S(2)}, u32[]{:S(2)}) %collective-permute-start.4) | collective-permute-done | bytes 524320 | tf_op jit(solution)/shard_map/ppermute | solution.py:327
  43.5 3.7 %update.1 = (bf16[2,512,1024]{2,1,0:T(8,128)(2,1)}, f32[8,128]{1,0:T(8,128)S(1)}) custom-call(f32[2,256,512]{2,1,0:T(8,128)S(1)} %get-tuple-element.23.mine_ref, bf16[2,256,512]{2,1,0:T(8,128)(2,1)S(1)} %collective-permute-done.4.theirs_ref, bf16[2,256,1024]{2,1,0:T(8,128)(2,1)S(1)} %get-tuple-element.19.inverse_ref, ...), custom_call_target="tpu_custom_call" | custom-call | flops 536 | bytes 8 | tf_op jit(solution)/shard_map/update/pallas_call | solution.py:43
  47.2 0.0 collective-permute-done.1.refs_0_
  47.2 0.5 collective-permute-start.5
  47.7 2.4 %landed.1.sofar_ref = f32[1,512,1024]{2,1,0:T(8,128)S(1)} custom-call(s32[256]{0:T(256)S(1)} %copy-done.6, bf16[528,1024]{1,0:T(8,128)(2,1)S(1)} %after.3.table_ref.pix_ref, bf16[528,1024]{1,0:T(8,128)(2,1)S(1)} %after.3.table_ref.pix_ref, f32[1,512,1024]{2,1,0:T(8,128)S(1)} %get-tuple-element.26.sofar_ref), custom_call_target="tpu_custom_call" | custom-call | flops 536 | bytes 8 | tf_op jit(solution)/shard_map/landed/pallas_call | solution.py:43
  50.1 0.0 collective-permute-done.5.table_ref.pix_ref
  50.1 3.5 %other.1 = f32[1,512,1024]{2,1,0:T(8,128)} custom-call(s32[256]{0:T(256)S(1)} %copy-done.6, bf16[528,1024]{1,0:T(8,128)(2,1)S(1)} %collective-permute-done.5.table_ref.pix_ref, bf16[528,1024]{1,0:T(8,128)(2,1)S(1)} %collective-permute-done.5.table_ref.pix_ref, f32[1,512,1024]{2,1,0:T(8,128)S(1)} %landed.1.sofar_ref), custom_call_target="tpu_custom_call" | custom-call | flops 536 | bytes 8 | tf_op jit(solution)/shard_map/other/pallas_call | solution.py:43
  (6 shorter events, 0.0 us)
Async XLA Ops:
  0.6 33.0 %collective-permute-start.2 = (bf16[1,512,1024]{2,1,0:T(8,128)(2,1)}, bf16[1,512,1024]{2,1,0:T(8,128)(2,1)S(1)}, u32[]{:S(2)}, u32[]{:S(2)}) collective-permute-start(bf16[1,512,1024]{2,1,0:T(8,128)(2,1)} %here_ref.1), channel_id=1, source_target_pairs={{0,2},{2,4},{4,6},{6,8},{8,10},{10,12},{12,14},{14,16},{16,18},{18... | collective-permute-start | bytes 3145736 | tf_op jit(solution)/shard_map/ppermute | solution.py:315
  3.8 30.8 %collective-permute-start.3 = (bf16[1,512,1024]{2,1,0:T(8,128)(2,1)}, bf16[1,512,1024]{2,1,0:T(8,128)(2,1)S(1)}, u32[]{:S(2)}, u32[]{:S(2)}) collective-permute-start(bf16[1,512,1024]{2,1,0:T(8,128)(2,1)} %here_ref.1), channel_id=1, source_target_pairs={{2,0},{4,2},{6,4},{8,6},{10,8},{12,10},{14,12},{16,14},{18,16},{20... | collective-permute-start | bytes 3145736 | tf_op jit(solution)/shard_map/ppermute | solution.py:316
  12.5 2.1 %collective-permute-start = (s32[2,512]{1,0:T(2,128)}, s32[2,512]{1,0:T(2,128)S(1)}, u32[]{:S(2)}, u32[]{:S(2)}) collective-permute-start(s32[2,512]{1,0:T(2,128)} %pix_ref.3), channel_id=1, source_target_pairs={{0,1},{1,0},{2,3},{3,2},{4,5},{5,4},{6,7},{7,6},{8,9},{9,8},{10,11... | collective-permute-start | bytes 12296 | tf_op jit(solution)/shard_map/ppermute | solution.py:317
  14.6 2.2 %copy-start = (bf16[2,1024,1024]{2,1,0:T(8,128)(2,1)S(1)}, bf16[2,1024,1024]{2,1,0:T(8,128)(2,1)}, u32[]{:S(2)}) copy-start(bf16[2,1024,1024]{2,1,0:T(8,128)(2,1)} %weights_ref.5) | copy-start | bytes 12582916
  16.7 1.2 %copy-start.2 = (bf16[2,1024,256]{2,1,0:T(8,128)(2,1)S(1)}, bf16[2,1024,256]{2,1,0:T(8,128)(2,1)}, u32[]{:S(2)}) copy-start(bf16[2,1024,256]{2,1,0:T(8,128)(2,1)} %leaf_ref.2) | copy-start | bytes 3145732
  18.0 0.7 %copy-start.4 = (s32[2,512]{1,0:T(2,128)S(1)}, s32[2,512]{1,0:T(2,128)}, u32[]{:S(2)}) copy-start(s32[2,512]{1,0:T(2,128)} %pix_ref.3) | copy-start | bytes 12292
  18.7 2.8 %copy-start.3 = (bf16[1,1024,256]{2,1,0:T(8,128)(2,1)S(1)}, bf16[1,1024,256]{2,1,0:T(8,128)(2,1)}, u32[]{:S(2)}) copy-start(bf16[1,1024,256]{2,1,0:T(8,128)(2,1)} %leaf_ref.3) | copy-start | bytes 1572868
  18.7 2.8 %copy-start.5 = (s32[2,512]{1,0:T(2,128)S(1)}, s32[2,512]{1,0:T(2,128)}, u32[]{:S(2)}) copy-start(s32[2,512]{1,0:T(2,128)} %pix_ref.3) | copy-start | bytes 12292
  18.7 2.8 %copy-start.6 = (s32[256]{0:T(256)S(1)}, s32[256]{0:T(256)}, u32[]{:S(2)}) copy-start(s32[256]{0:T(256)} %ids_ref.7) | copy-start | bytes 3076
  18.7 2.8 %copy-start.7 = (s32[1,512]{1,0:T(1,128)S(1)}, s32[1,512]{1,0:T(1,128)}, u32[]{:S(2)}) copy-start(s32[1,512]{1,0:T(1,128)} %parent_pix_ref.1) | copy-start | bytes 6148
  21.5 13.1 %copy-start.1 = (bf16[2,1024,1024]{2,1,0:T(8,128)(2,1)S(1)}, bf16[2,1024,1024]{2,1,0:T(8,128)(2,1)}, u32[]{:S(2)}) copy-start(bf16[2,1024,1024]{2,1,0:T(8,128)(2,1)} %weights_ref.5) | copy-start | bytes 12582916
  21.5 13.1 %copy-start.8 = (bf16[1,512,1024]{2,1,0:T(8,128)(2,1)S(1)}, bf16[1,512,1024]{2,1,0:T(8,128)(2,1)}, u32[]{:S(2)}) copy-start(bf16[1,512,1024]{2,1,0:T(8,128)(2,1)} %here_ref.1) | copy-start | bytes 3145732
  26.1 21.1 %collective-permute-start.1 = (bf16[528,1024]{1,0:T(8,128)(2,1)S(1)}, bf16[528,1024]{1,0:T(8,128)(2,1)S(1)}, u32[]{:S(2)}, u32[]{:S(2)}) collective-permute-start(bf16[528,1024]{1,0:T(8,128)(2,1)S(1)} %after.2), channel_id=1, source_target_pairs={{0,2},{2,4},{4,6},{6,8},{8,10},{10,12},{12,14},{14,16},{16,18},{18... | collective-permute-start | bytes 3244040 | tf_op jit(solution)/shard_map/ppermute | solution.py:323
  39.2 4.2 %collective-permute-start.4 = (bf16[2,256,512]{2,1,0:T(8,128)(2,1)S(1)}, bf16[2,256,512]{2,1,0:T(8,128)(2,1)S(1)}, u32[]{:S(2)}, u32[]{:S(2)}) collective-permute-start(bf16[2,256,512]{2,1,0:T(8,128)(2,1)S(1)} %get-tuple-element.24), channel_id=1, source_target_pairs={{0,1},{1,0},{2,3},{3,2},{4,5},{5,4},{6,7},{7,6},{8,9},{9,8},{10,11... | collective-permute-start | bytes 1572872 | tf_op jit(solution)/shard_map/ppermute | solution.py:327
  47.2 2.9 %collective-permute-start.5 = (bf16[528,1024]{1,0:T(8,128)(2,1)S(1)}, bf16[528,1024]{1,0:T(8,128)(2,1)S(1)}, u32[]{:S(2)}, u32[]{:S(2)}) collective-permute-start(bf16[528,1024]{1,0:T(8,128)(2,1)S(1)} %after.3.table_ref.pix_ref), channel_id=1, source_target_pairs={{0,1},{1,0},{2,3},{3,2},{4,5},{5,4},{6,7},{7,6},{8,9},{9,8},{10,11... | collective-permute-start | bytes 3244040 | tf_op jit(solution)/shard_map/ppermute | solution.py:330
